TPU v7x, 32 devices: a whole 2x2x4 slice. The times are simulated.
32 devices in a mesh: row: 2 (over y), col: 4 (over x, core), layer: 4 (over z).
Axes of the slice: x: 2, y: 2, z: 4, core: 2. Of those that a mesh axis runs over, the one named last changes fastest.
Arguments:
- coeffs: float32 [4096, 4096], P(('row', 'col'), 'layer'), may hold values from -6 to 6
- hblocks: float32 [256, 128, 128], P('layer'), may hold values from -0.1875 to 0.1875
- hcount: int32 [32], replicated, may hold values from 1 to 16, 256 in all
- hcols: int32 [256], P('layer'), may hold values from 0 to 31
Outputs:
- sigma: float32 [4096, 4096], P(('row', 'col'), 'layer')
Inputs may be any that keep to these rules, and one draw needn't show every extreme that they name: `hcount`: the blocks of a row stand together in hcols and hblocks, rows in order; the counts sum to 256 and some row holds 16. `hcols`: a row may name a column more than once; such blocks add.
All inputs are finite; a program needn't handle non-finite values.
Results may differ from a plain program's by a relative error of at most 0.00007.
Values sent between devices are 32-bit elements; how exact they have to be, the bound alone decides.
A program may use at most 128 MiB of HBM per device.

v0:
```python
import functools

import jax
import jax.numpy as jnp
from jax import lax
from jax.experimental import pallas as pl
from jax.experimental.pallas import tpu as pltpu
from jax.sharding import PartitionSpec as P

MESH = pl.DeviceIdType.MESH
ANY = pl.BlockSpec(memory_space=pl.ANY)


def place():
    return lax.axis_index("row"), lax.axis_index("col"), lax.axis_index("layer")


def plane_peer(sizes, row, col, offset):
    rows, cols, _ = sizes
    down, right = offset // cols, offset % cols
    to = (lax.rem(row + down, rows), lax.rem(col + right, cols))
    source = lax.rem(row + rows - down, rows) * cols + lax.rem(col + cols - right, cols)
    return to, source


def greet(sizes):
    rows, cols, layers = sizes
    row, col, layer = place()
    barrier = pltpu.get_barrier_semaphore()
    for k in range(1, layers):
        to = (row, col, lax.rem(layer + k, layers))
        pl.semaphore_signal(barrier, inc=1, device_id=to, device_id_type=MESH)
    for offset in range(1, rows * cols):
        to, _ = plane_peer(sizes, row, col, offset)
        pl.semaphore_signal(barrier, inc=1, device_id=(*to, layer), device_id_type=MESH)
    pl.semaphore_wait(barrier, layers - 1 + rows * cols - 1)


def remote(src, dst, send_sem, recv_sem, to):
    return pltpu.make_async_remote_copy(
        src_ref=src,
        dst_ref=dst,
        send_sem=send_sem,
        recv_sem=recv_sem,
        device_id=to,
        device_id_type=MESH,
    )


def exchange(sizes, by_layer, by_plane, to_layer, to_plane, sems):
    rows, cols, layers = sizes
    row, col, layer = place()
    layer_send, layer_recv, plane_send, plane_recv = sems
    over_layer, over_plane = [], []
    for k in range(1, layers):
        other = lax.rem(layer + k, layers)
        over_layer.append(
            remote(
                by_layer.at[other],
                to_layer.at[layer],
                layer_send.at[k],
                layer_recv.at[k],
                (row, col, other),
            )
        )
    me = row * cols + col
    for offset in range(1, rows * cols):
        to, _ = plane_peer(sizes, row, col, offset)
        over_plane.append(
            remote(
                by_plane.at[to[0] * cols + to[1]],
                to_plane.at[me],
                plane_send.at[offset],
                plane_recv.at[offset],
                (*to, layer),
            )
        )
    return over_layer, over_plane


def out_kernel(
    sizes,
    c_ref,
    t_ref,
    h_ref,
    k_ref,
    z_ref,
    x_ref,
    all_ref,
    cols_ref,
    own_sem,
    layer_send,
    layer_recv,
    plane_send,
    plane_recv,
    cols_send,
    cols_recv,
    rise_send,
    fall_send,
    relay_recv,
    chip_send,
    chip_recv,
    pair_send,
    pair_recv,
):
    rows, cols, layers = sizes
    row, col, layer = place()
    me = row * cols + col
    step = 2 if cols % 2 == 0 else 1
    offsets = [d * cols + e for d in range(rows) for e in range(0, cols, step)]

    greet(sizes)

    def relay(piece, up):
        src = h_ref.at[me] if piece is None else all_ref.at[piece, me]
        piece = layer if piece is None else piece
        sem = rise_send if up else fall_send
        to = (row, col, layer + 1 if up else layer - 1)
        return remote(src, all_ref.at[piece, me], sem.at[piece], relay_recv.at[piece], to)

    def to_chips(piece):
        made = []
        for at, offset in enumerate(offsets[1:]):
            to, _ = plane_peer(sizes, row, col, offset)
            made.append(
                remote(
                    all_ref.at[piece, me],
                    all_ref.at[piece, me],
                    chip_send.at[piece, at],
                    chip_recv.at[piece, at],
                    (*to, layer),
                )
            )
        return made

    def to_pair(piece, at):
        _, source = plane_peer(sizes, row, col, offsets[at])
        twin = (row, col + 1 - 2 * lax.rem(col, 2), layer)
        return remote(
            all_ref.at[piece, source],
            all_ref.at[piece, source],
            pair_send.at[piece, at],
            pair_recv.at[piece, at],
            twin,
        )

    def each_piece(k, act):
        @pl.when(layer >= k)
        def below():
            act(layer - k, True)

        @pl.when(layer + k < layers)
        def above():
            act(layer + k, False)

    can_rise, can_fall = layer + 1 < layers, layer > 0

    @pl.when(can_rise)
    def rise():
        relay(None, True).start()

    @pl.when(can_fall)
    def fall():
        relay(None, False).start()

    over_layer, over_plane = exchange(
        sizes, c_ref, t_ref, z_ref, x_ref, (layer_send, layer_recv, plane_send, plane_recv)
    )
    names = []
    for k in range(1, layers):
        to = (row, col, lax.rem(layer + k, layers))
        names.append(remote(k_ref, cols_ref.at[layer], cols_send.at[k], cols_recv.at[k], to))
    own = [
        pltpu.make_async_copy(c_ref.at[layer], z_ref.at[layer], own_sem.at[0]),
        pltpu.make_async_copy(t_ref.at[me], x_ref.at[me], own_sem.at[1]),
        pltpu.make_async_copy(h_ref, all_ref.at[layer], own_sem.at[2]),
        pltpu.make_async_copy(k_ref, cols_ref.at[layer], own_sem.at[3]),
    ]
    for copy in names + over_plane + own:
        copy.start()

    def arrive(piece, upward):
        relay(piece, upward).wait_recv()

        @pl.when(can_rise if upward else can_fall)
        def onward():
            relay(piece, upward).start()

        for copy in to_chips(piece):
            copy.start()
        if step == 2:
            to_pair(piece, 0).start()

    late = min(2, layers - 1)
    for k in range(1, layers):
        each_piece(k, arrive)
        if k == late:
            for copy in over_layer:
                copy.start()
    if layers == 1:
        for copy in over_layer:
            copy.start()

    def pass_on(piece, upward):
        for at, copy in enumerate(to_chips(piece)):
            copy.wait_recv()
            if step == 2:
                to_pair(piece, at + 1).start()

    for k in range(1, layers):
        each_piece(k, pass_on)

    def finish(piece, upward):
        @pl.when(can_rise if upward else can_fall)
        def sent():
            relay(piece, upward).wait_send()

        for copy in to_chips(piece):
            copy.wait_send()
        if step == 2:
            for at in range(len(offsets)):
                copy = to_pair(piece, at)
                copy.wait_send()
                copy.wait_recv()

    for k in range(1, layers):
        each_piece(k, finish)

    @pl.when(can_rise)
    def risen():
        relay(None, True).wait_send()

    @pl.when(can_fall)
    def fallen():
        relay(None, False).wait_send()

    for copy in names + over_plane + over_layer + own:
        copy.wait()


def back_kernel(
    sizes,
    b_ref,
    a_ref,
    beta_ref,
    alpha_ref,
    own_sem,
    layer_send,
    layer_recv,
    plane_send,
    plane_recv,
):
    rows, cols, layers = sizes
    row, col, layer = place()
    me = row * cols + col
    greet(sizes)
    over_layer, over_plane = exchange(
        sizes, b_ref, a_ref, beta_ref, alpha_ref, (layer_send, layer_recv, plane_send, plane_recv)
    )
    own = [
        pltpu.make_async_copy(b_ref.at[layer], beta_ref.at[layer], own_sem.at[0]),
        pltpu.make_async_copy(a_ref.at[me], alpha_ref.at[me], own_sem.at[1]),
    ]
    for copy in over_layer + over_plane + own:
        copy.start()
    for copy in over_layer + over_plane + own:
        copy.wait()


def halves(values):
    high = values.astype(jnp.bfloat16)
    low = (values - high.astype(jnp.float32)).astype(jnp.bfloat16)
    return high, low


def product_kernel(owner_ref, column_ref, z_ref, x_ref, h_ref, a_ref, b_ref, y_ref):
    chunk, block = h_ref.shape[0], h_ref.shape[1]
    blocks, alpha_rows, _ = a_ref.shape
    step = pl.program_id(0)

    @pl.when(step == 0)
    def prepare():
        a_ref[...] = jnp.zeros_like(a_ref)
        b_ref[...] = jnp.zeros_like(b_ref)
        for ref, low_row in ((x_ref, 0), (z_ref, alpha_rows)):
            per = ref.shape[2] // block
            count = ref.shape[1]
            for j in range(blocks):
                part = ref[j // per, :, (j % per) * block : (j % per + 1) * block]
                high, low = halves(part)
                y_ref[j, low_row : low_row + count, :block] = high
                y_ref[j, low_row : low_row + count, block:] = low

    group = 4

    def body(at, carry):
        results = []
        for i in range(group):
            n = at * group + i
            high, low = halves(h_ref[n])
            weights = jnp.concatenate(
                [jnp.concatenate([high, high], axis=1), jnp.concatenate([low, low], axis=1)], axis=0
            )
            picked = y_ref[column_ref[step * chunk + n]]
            both = lax.dot_general(
                picked, weights, (((1,), (1,)), ((), ())), preferred_element_type=jnp.float32
            )
            results.append(both[:, :block] + both[:, block:])
        for i in range(group):
            owner = owner_ref[step * chunk + at * group + i]
            a_ref[owner] += results[i][:alpha_rows]
            b_ref[owner] += results[i][alpha_rows:]
        return carry

    lax.fori_loop(0, chunk // group, body, 0)


def local(sizes, coeffs, hblocks, hcount, hcols):
    rows, cols, layers = sizes
    group = rows * cols
    row_count, col_count = coeffs.shape
    share, block, _ = hblocks.shape
    stored = share * layers
    blocks = row_count * group // block
    alpha_rows, beta_rows = col_count // group, row_count // layers
    f32 = jnp.float32
    dma = pltpu.SemaphoreType.DMA

    padded = -(-share // 1024) * 1024
    names = jnp.pad(hcols, (0, padded - share)).reshape(-1, 128)
    flipped = coeffs.T.reshape(group, alpha_rows, row_count)
    chips = group // 2 if cols % 2 == 0 else group
    z, x, everything, columns = pl.pallas_call(
        functools.partial(out_kernel, sizes),
        out_shape=(
            jax.ShapeDtypeStruct((layers, beta_rows, col_count), f32),
            jax.ShapeDtypeStruct((group, alpha_rows, row_count), f32),
            jax.ShapeDtypeStruct((layers, group, share // group, block, block), f32),
            jax.ShapeDtypeStruct((layers, *names.shape), jnp.int32),
        ),
        in_specs=[ANY] * 4,
        out_specs=(ANY,) * 4,
        scratch_shapes=[dma((4,))]
        + [dma((layers,))] * 2
        + [dma((group,))] * 2
        + [dma((layers,))] * 5
        + [dma((layers, chips))] * 4,
        compiler_params=pltpu.CompilerParams(collective_id=0, has_side_effects=True),
        name="spread",
    )(
        coeffs.reshape(layers, beta_rows, col_count),
        flipped,
        hblocks.reshape(group, share // group, block, block),
        names,
    )

    row_end = jnp.cumsum(hcount)
    index = jnp.arange(stored, dtype=jnp.int32)
    owners = jnp.sum((row_end[None, :] <= index[:, None]).astype(jnp.int32), axis=1)
    columns = columns.reshape(layers, -1)[:, :share].reshape(stored)
    chunk = 16
    whole = lambda shape: pl.BlockSpec(shape, lambda i, *_: (0,) * len(shape))
    a_shape, b_shape = (blocks, alpha_rows, block), (blocks, beta_rows, block)
    alpha, beta = pl.pallas_call(
        product_kernel,
        out_shape=(jax.ShapeDtypeStruct(a_shape, f32), jax.ShapeDtypeStruct(b_shape, f32)),
        grid_spec=pltpu.PrefetchScalarGridSpec(
            num_scalar_prefetch=2,
            grid=(stored // chunk,),
            in_specs=[
                whole(z.shape),
                whole(x.shape),
                pl.BlockSpec((chunk, block, block), lambda i, *_: (i, 0, 0)),
            ],
            out_specs=(whole(a_shape), whole(b_shape)),
            scratch_shapes=[pltpu.VMEM((blocks, alpha_rows + beta_rows, 2 * block), jnp.bfloat16)],
        ),
        compiler_params=pltpu.CompilerParams(vmem_limit_bytes=48 * 2**20),
        name="product",
    )(owners, columns, z, x, everything.reshape(stored, block, block))

    per_layer, per_plane = blocks // layers, blocks // group
    beta_back = (layers, per_layer, beta_rows, block)
    alpha_back = (group, per_plane, alpha_rows, block)
    beta, alpha = pl.pallas_call(
        functools.partial(back_kernel, sizes),
        out_shape=(jax.ShapeDtypeStruct(beta_back, f32), jax.ShapeDtypeStruct(alpha_back, f32)),
        in_specs=[ANY] * 2,
        out_specs=(ANY,) * 2,
        scratch_shapes=[dma((2,))] + [dma((layers,))] * 2 + [dma((group,))] * 2,
        compiler_params=pltpu.CompilerParams(collective_id=1, has_side_effects=True),
        name="collect",
    )(beta.reshape(beta_back), alpha.reshape(alpha_back))
    beta = beta.transpose(0, 2, 1, 3).reshape(row_count, col_count)
    alpha = alpha.transpose(1, 3, 0, 2).reshape(row_count, col_count)
    return beta + alpha


def solution(mesh):
    sizes = tuple(mesh.shape[name] for name in ("row", "col", "layer"))
    in_specs = (P(("row", "col"), "layer"), P("layer", None, None), P(), P("layer"))
    out_specs = P(("row", "col"), "layer")
    return jax.shard_map(
        functools.partial(local, sizes),
        mesh=mesh,
        in_specs=in_specs,
        out_specs=out_specs,
        check_vma=False,
    )
```

profile of v0, /device:TPU:26, one launch (start us, length us, event | category | flops | bytes accessed | tf_op | source)
XLA Modules:
  0.0 248.1 jit_solution(2793705583116465868)
XLA Ops:
  0.0 1.2 pad_bitcast_fusion.k_ref
  1.3 0.7 copy.12
  2.0 0.1 reduce-window.8
  2.0 0.1 reduce
  2.2 0.1 convert_reduce_fusion.owner_ref
  2.3 2.9 %copy.13 = f32[1024,512]{1,0:T(8,128)} copy(f32[1024,512]{0,1:T(8,128)} %bitcast.27) | data formatting | bytes 4194304 | tf_op jit(solution)/shard_map/transpose | solution.py:331
  5.1 154.6 %spread.1 = (f32[4,128,1024]{2,1,0:T(8,128)}, f32[8,128,512]{2,1,0:T(8,128)}, f32[4,8,8,128,128]{4,3,2,1,0:T(8,128)}, s32[4,8,128]{2,1,0:T(8,128)}) custom-call(f32[4,128,1024]{2,1,0:T(8,128)} %bitcast.28, f32[8,128,512]{2,1,0:T(8,128)} %bitcast.29, f32[8,8,128,128]{3,2,1,0:T(8,128)} %bitcast.30, s32[8,128]{1,0:T(8,128)} %pad_bitcast_fusion.k_ref), custom_call_target="tpu_custom_call" | custom-call | tf_op jit(solution)/shard_map/spread/pallas_call | solution.py:333
  159.8 0.7 copy.21
  160.5 0.1 reshape.63.column_ref
  160.6 26.4 %product.1 = (f32[32,128,128]{2,1,0:T(8,128)S(1)}, f32[32,128,128]{2,1,0:T(8,128)S(1)}) custom-call(s32[256]{0:T(256)S(1)} %convert_reduce_fusion.owner_ref, s32[256]{0:T(256)S(1)} %reshape.63.column_ref, f32[4,128,1024]{2,1,0:T(8,128)} %get-tuple-element.14.z_ref, f32[8,128,512]{2,1,0:T(8,128)} %get-tuple-element.15.x_ref, f32[256,128,128]{2,1,0:T(8,128)} %bitcast.25), custom_call_target="tpu_custom_call" | custom-call | tf_op jit(solution)/shard_map/product/pallas_call | solution.py:364
  187.0 0.0 copy-start
  187.0 1.3 copy-done
  188.4 0.0 copy-start.1
  188.4 1.3 copy-done.1
  189.7 49.4 %collect.1 = (f32[4,8,128,128]{3,2,1,0:T(8,128)}, f32[8,4,128,128]{3,2,1,0:T(8,128)}) custom-call(f32[4,8,128,128]{3,2,1,0:T(8,128)} %bitcast.24, f32[8,4,128,128]{3,2,1,0:T(8,128)} %bitcast.23), custom_call_target="tpu_custom_call" | custom-call | tf_op jit(solution)/shard_map/collect/pallas_call | solution.py:385
  239.1 1.9 copy.14
  241.1 3.2 %bitcast_add_fusion = f32[4,128,8,128]{1,3,0,2:T(8,128)} fusion(f32[8,4,128,128]{3,2,1,0:T(8,128)} %get-tuple-element.20, f32[4,8,128,128]{2,3,0,1:T(8,128)S(1)} %copy.14), kind=kLoop, calls=%fused_computation.1 | loop fusion | flops 524288 | bytes 6291456 | tf_op jit(solution)/shard_map/add | solution.py:396
  244.3 2.0 copy.15
  246.3 1.8 copy.20
  (1 shorter events, 0.0 us)
Async XLA Ops:
  187.0 1.4 copy-start
  188.4 1.3 copy-start.1
where the time goes:
time: 250 us; the launch traced here: 248 us
  Pallas kernels  231 us (92%)
  local copies, waits for them, and re-layouts  14.1 us (6%)
  other arithmetic  3.42 us (1%)
    pallas_call x1, Pallas kernels, local(): pl.pallas_call(functools.partial(out_kernel, sizes), out_shape=(jax.Shape...  155 us
    pallas_call x1, Pallas kernels, local(): pl.pallas_call(functools.partial(back_kernel, sizes), out_shape=(jax.Shap...  49.4 us
    pallas_call x1, Pallas kernels, local(): pl.pallas_call(product_kernel, out_shape=(jax.ShapeDtypeStruct(a_shape, f...  26.4 us
    unnamed x6, local copies, waits for them, and re-layouts  5.17 us

commit v1 on v0

--- a/solution.py
+++ b/solution.py
@@ -108,6 +108,8 @@
     me = row * cols + col
     step = 2 if cols % 2 == 0 else 1
     offsets = [d * cols + e for d in range(rows) for e in range(0, cols, step)]
+    half = h_ref.shape[1] // 2
+    square = rows == 2 and cols == 4 and half > 0
 
     greet(sizes)
 
@@ -118,20 +120,22 @@
         to = (row, col, layer + 1 if up else layer - 1)
         return remote(src, all_ref.at[piece, me], sem.at[piece], relay_recv.at[piece], to)
 
-    def to_chips(piece):
-        made = []
-        for at, offset in enumerate(offsets[1:]):
-            to, _ = plane_peer(sizes, row, col, offset)
-            made.append(
-                remote(
-                    all_ref.at[piece, me],
-                    all_ref.at[piece, me],
-                    chip_send.at[piece, at],
-                    chip_recv.at[piece, at],
-                    (*to, layer),
-                )
-            )
-        return made
+    def to_chip(piece, at):
+        to, _ = plane_peer(sizes, row, col, offsets[at])
+        return remote(
+            all_ref.at[piece, me],
+            all_ref.at[piece, me],
+            chip_send.at[piece, at],
+            chip_recv.at[piece, at],
+            (*to, layer),
+        )
+
+    def to_corner(piece, part):
+        _, source = plane_peer(sizes, row, col, offsets[1 + part])
+        to, _ = plane_peer(sizes, row, col, offsets[2 - part])
+        block = all_ref.at[piece, source, pl.ds(part * half, half)]
+        at = 0 if part == 0 else 3
+        return remote(block, block, chip_send.at[piece, at], chip_recv.at[piece, at], (*to, layer))
 
     def to_pair(piece, at):
         _, source = plane_peer(sizes, row, col, offsets[at])
@@ -144,6 +148,8 @@
             twin,
         )
 
+    chips = [1, 2] if square else list(range(1, len(offsets)))
+
     def each_piece(k, act):
         @pl.when(layer >= k)
         def below():
@@ -173,8 +179,7 @@
     own = [
         pltpu.make_async_copy(c_ref.at[layer], z_ref.at[layer], own_sem.at[0]),
         pltpu.make_async_copy(t_ref.at[me], x_ref.at[me], own_sem.at[1]),
-        pltpu.make_async_copy(h_ref, all_ref.at[layer], own_sem.at[2]),
-        pltpu.make_async_copy(k_ref, cols_ref.at[layer], own_sem.at[3]),
+        pltpu.make_async_copy(k_ref, cols_ref.at[layer], own_sem.at[2]),
     ]
     for copy in names + over_plane + own:
         copy.start()
@@ -186,37 +191,49 @@
         def onward():
             relay(piece, upward).start()
 
-        for copy in to_chips(piece):
-            copy.start()
+        for at in chips:
+            to_chip(piece, at).start()
         if step == 2:
             to_pair(piece, 0).start()
 
-    late = min(2, layers - 1)
+    def pass_on(piece, upward):
+        for at in chips:
+            to_chip(piece, at).wait_recv()
+            if square:
+                to_corner(piece, at - 1).start()
+            if step == 2:
+                to_pair(piece, at).start()
+
+    def pass_corner(piece, upward):
+        if square:
+            to_corner(piece, 0).wait_recv()
+            to_corner(piece, 1).wait_recv()
+            to_pair(piece, 3).start()
+
     for k in range(1, layers):
         each_piece(k, arrive)
-        if k == late:
-            for copy in over_layer:
-                copy.start()
-    if layers == 1:
-        for copy in over_layer:
-            copy.start()
-
-    def pass_on(piece, upward):
-        for at, copy in enumerate(to_chips(piece)):
-            copy.wait_recv()
-            if step == 2:
-                to_pair(piece, at + 1).start()
-
-    for k in range(1, layers):
-        each_piece(k, pass_on)
+        if k > 1 and k < layers - 1:
+            each_piece(k - 1, pass_on)
+    for copy in over_layer:
+        copy.start()
+    if layers > 2:
+        each_piece(layers - 2, pass_on)
+        each_piece(1, pass_corner) if layers > 3 else None
+    if layers > 1:
+        each_piece(layers - 1, pass_on)
+    for k in range(2 if layers > 3 else 1, layers):
+        each_piece(k, pass_corner)
 
     def finish(piece, upward):
         @pl.when(can_rise if upward else can_fall)
         def sent():
             relay(piece, upward).wait_send()
 
-        for copy in to_chips(piece):
-            copy.wait_send()
+        for at in chips:
+            to_chip(piece, at).wait_send()
+        if square:
+            to_corner(piece, 0).wait_send()
+            to_corner(piece, 1).wait_send()
         if step == 2:
             for at in range(len(offsets)):
                 copy = to_pair(piece, at)
@@ -273,8 +290,11 @@
     return high, low
 
 
-def product_kernel(owner_ref, column_ref, z_ref, x_ref, h_ref, a_ref, b_ref, y_ref):
+def product_kernel(
+    own_steps, owner_ref, column_ref, first_ref, z_ref, x_ref, own_ref, h_ref, a_ref, b_ref, y_ref
+):
     chunk, block = h_ref.shape[0], h_ref.shape[1]
+    stored = owner_ref.shape[0]
     blocks, alpha_rows, _ = a_ref.shape
     step = pl.program_id(0)
 
@@ -291,28 +311,43 @@
                 y_ref[j, low_row : low_row + count, :block] = high
                 y_ref[j, low_row : low_row + count, block:] = low
 
+    start = lax.rem(first_ref[0] + step * chunk, stored)
     group = 4
 
-    def body(at, carry):
-        results = []
-        for i in range(group):
-            n = at * group + i
-            high, low = halves(h_ref[n])
-            weights = jnp.concatenate(
-                [jnp.concatenate([high, high], axis=1), jnp.concatenate([low, low], axis=1)], axis=0
-            )
-            picked = y_ref[column_ref[step * chunk + n]]
-            both = lax.dot_general(
-                picked, weights, (((1,), (1,)), ((), ())), preferred_element_type=jnp.float32
-            )
-            results.append(both[:, :block] + both[:, block:])
-        for i in range(group):
-            owner = owner_ref[step * chunk + at * group + i]
-            a_ref[owner] += results[i][:alpha_rows]
-            b_ref[owner] += results[i][alpha_rows:]
-        return carry
-
-    lax.fori_loop(0, chunk // group, body, 0)
+    def run(ref):
+        def body(at, carry):
+            results = []
+            for i in range(group):
+                n = at * group + i
+                high, low = halves(ref[n])
+                weights = jnp.concatenate(
+                    [
+                        jnp.concatenate([high, high], axis=1),
+                        jnp.concatenate([low, low], axis=1),
+                    ],
+                    axis=0,
+                )
+                picked = y_ref[column_ref[start + n]]
+                both = lax.dot_general(
+                    picked, weights, (((1,), (1,)), ((), ())), preferred_element_type=jnp.float32
+                )
+                results.append(both[:, :block] + both[:, block:])
+            for i in range(group):
+                owner = owner_ref[start + at * group + i]
+                a_ref[owner] += results[i][:alpha_rows]
+                b_ref[owner] += results[i][alpha_rows:]
+            return carry
+
+        lax.fori_loop(0, chunk // group, body, 0)
+
+    pl.when(step < own_steps)(lambda: run(own_ref))
+    pl.when(step >= own_steps)(lambda: run(h_ref))
+
+
+def join_kernel(b_ref, a_ref, out_ref):
+    block = b_ref.shape[-1]
+    for p in range(b_ref.shape[1]):
+        out_ref[:, p * block : (p + 1) * block] = b_ref[0, p] + a_ref[p, 0].T
 
 
 def local(sizes, coeffs, hblocks, hcount, hcols):
@@ -340,7 +375,7 @@
         ),
         in_specs=[ANY] * 4,
         out_specs=(ANY,) * 4,
-        scratch_shapes=[dma((4,))]
+        scratch_shapes=[dma((3,))]
         + [dma((layers,))] * 2
         + [dma((group,))] * 2
         + [dma((layers,))] * 5
@@ -359,25 +394,36 @@
     owners = jnp.sum((row_end[None, :] <= index[:, None]).astype(jnp.int32), axis=1)
     columns = columns.reshape(layers, -1)[:, :share].reshape(stored)
     chunk = 16
+    own_steps, steps = share // chunk, stored // chunk
+    first = jnp.reshape(lax.axis_index("layer") * share, (1,)).astype(jnp.int32)
     whole = lambda shape: pl.BlockSpec(shape, lambda i, *_: (0,) * len(shape))
+
+    def own_at(i, owner_ref, column_ref, first_ref):
+        return jnp.minimum(i, own_steps - 1), 0, 0
+
+    def other_at(i, owner_ref, column_ref, first_ref):
+        later = jnp.maximum(i, min(own_steps, steps - 1))
+        return lax.rem(first_ref[0] // chunk + later, steps), 0, 0
+
     a_shape, b_shape = (blocks, alpha_rows, block), (blocks, beta_rows, block)
     alpha, beta = pl.pallas_call(
-        product_kernel,
+        functools.partial(product_kernel, own_steps),
         out_shape=(jax.ShapeDtypeStruct(a_shape, f32), jax.ShapeDtypeStruct(b_shape, f32)),
         grid_spec=pltpu.PrefetchScalarGridSpec(
-            num_scalar_prefetch=2,
-            grid=(stored // chunk,),
+            num_scalar_prefetch=3,
+            grid=(steps,),
             in_specs=[
                 whole(z.shape),
                 whole(x.shape),
-                pl.BlockSpec((chunk, block, block), lambda i, *_: (i, 0, 0)),
+                pl.BlockSpec((chunk, block, block), own_at),
+                pl.BlockSpec((chunk, block, block), other_at),
             ],
             out_specs=(whole(a_shape), whole(b_shape)),
             scratch_shapes=[pltpu.VMEM((blocks, alpha_rows + beta_rows, 2 * block), jnp.bfloat16)],
         ),
         compiler_params=pltpu.CompilerParams(vmem_limit_bytes=48 * 2**20),
         name="product",
-    )(owners, columns, z, x, everything.reshape(stored, block, block))
+    )(owners, columns, first, z, x, hblocks, everything.reshape(stored, block, block))
 
     per_layer, per_plane = blocks // layers, blocks // group
     beta_back = (layers, per_layer, beta_rows, block)
@@ -391,6 +437,18 @@
         compiler_params=pltpu.CompilerParams(collective_id=1, has_side_effects=True),
         name="collect",
     )(beta.reshape(beta_back), alpha.reshape(alpha_back))
+    if alpha_rows == block and beta_rows == block:
+        return pl.pallas_call(
+            join_kernel,
+            out_shape=jax.ShapeDtypeStruct((row_count, col_count), f32),
+            grid=(layers,),
+            in_specs=[
+                pl.BlockSpec((1, per_layer, block, block), lambda i: (i, 0, 0, 0)),
+                pl.BlockSpec((group, 1, block, block), lambda i: (0, i, 0, 0)),
+            ],
+            out_specs=pl.BlockSpec((block, col_count), lambda i: (i, 0)),
+            name="join",
+        )(beta, alpha)
     beta = beta.transpose(0, 2, 1, 3).reshape(row_count, col_count)
     alpha = alpha.transpose(1, 3, 0, 2).reshape(row_count, col_count)
     return beta + alpha

time: 250 us -> 187 us (0.75)
  Pallas kernels: 231 us -> 177 us
  local copies, waits for them, and re-layouts: 14.1 us -> 8.34 us
  other arithmetic: 3.42 us -> 0.26 us
    pallas_call x1, Pallas kernels: 155 us -> 96.9 us  [local(): pl.pallas_call(functools.partial(out_kernel, sizes), out_shape=(jax.Shape...]
    pallas_call x1 -> x2, Pallas kernels: 26.4 us -> 31.7 us  [the longest x1 27.3 us: local(): pl.pallas_call(functools.partial(product_kernel, own_steps), out_shape=(j...]
    add x1 -> x0, other arithmetic: 3.16 us -> none  [local(): return beta + alpha]
    unnamed x6 -> x5, local copies, waits for them, and re-layouts: 5.17 us -> 3.39 us
where the time goes in v1:
time: 187 us; the launch traced here: 186 us
  Pallas kernels  177 us (95%)
  local copies, waits for them, and re-layouts  8.34 us (4%)
    pallas_call x1, Pallas kernels, local(): pl.pallas_call(functools.partial(out_kernel, sizes), out_shape=(jax.Shape...  96.9 us
    pallas_call x1, Pallas kernels, local(): pl.pallas_call(functools.partial(back_kernel, sizes), out_shape=(jax.Shap...  48.8 us
    pallas_call x1, Pallas kernels, local(): pl.pallas_call(functools.partial(product_kernel, own_steps), out_shape=(j...  27.3 us
    pallas_call x1, Pallas kernels, local(): pl.pallas_call(join_kernel, out_shape=jax.ShapeDtypeStruct((row_count, co...  4.48 us

profile of v1, /device:TPU:26, one launch (start us, length us, event | category | flops | bytes accessed | tf_op | source)
XLA Modules:
  0.0 186.0 jit_solution(6839120121866081547)
XLA Ops:
  0.0 1.2 pad_bitcast_fusion.k_ref
  1.3 0.7 copy.9
  2.0 0.1 reduce-window.8
  2.0 0.1 reduce
  2.2 0.1 convert_reduce_fusion.owner_ref
  2.3 2.9 %copy.10 = f32[1024,512]{1,0:T(8,128)} copy(f32[1024,512]{0,1:T(8,128)} %bitcast.19) | data formatting | bytes 4194304 | tf_op jit(solution)/shard_map/transpose | solution.py:366
  5.1 96.9 %spread.1 = (f32[4,128,1024]{2,1,0:T(8,128)}, f32[8,128,512]{2,1,0:T(8,128)}, f32[4,8,8,128,128]{4,3,2,1,0:T(8,128)}, s32[4,8,128]{2,1,0:T(8,128)}) custom-call(f32[4,128,1024]{2,1,0:T(8,128)} %bitcast.20, f32[8,128,512]{2,1,0:T(8,128)} %bitcast.21, f32[8,8,128,128]{3,2,1,0:T(8,128)} %bitcast.18, s32[8,128]{1,0:T(8,128)} %pad_bitcast_fusion.k_ref), custom_call_target="tpu_custom_call" | custom-call | tf_op jit(solution)/shard_map/spread/pallas_call | solution.py:368
  102.0 0.7 copy.13
  102.7 0.1 reshape.61.column_ref
  102.8 27.3 %product.1 = (f32[32,128,128]{2,1,0:T(8,128)S(1)}, f32[32,128,128]{2,1,0:T(8,128)S(1)}) custom-call(s32[256]{0:T(256)S(1)} %convert_reduce_fusion.owner_ref, s32[256]{0:T(256)S(1)} %reshape.61.column_ref, s32[1]{0:T(128)} %bitcast.6.first_ref, f32[4,128,1024]{2,1,0:T(8,128)} %get-tuple-element.14.z_ref, f32[8,128,512]{2,1,0:T(8,128)} %get-tuple-element.15.x_ref, ...), custom_call_target="tpu_custom_call" | custom-call | tf_op jit(solution)/shard_map/product/pallas_call | solution.py:409
  130.1 0.0 copy-start
  130.1 1.3 copy-done
  131.5 0.0 copy-start.1
  131.5 1.3 copy-done.1
  132.8 48.8 %collect.1 = (f32[4,8,128,128]{3,2,1,0:T(8,128)}, f32[8,4,128,128]{3,2,1,0:T(8,128)}) custom-call(f32[4,8,128,128]{3,2,1,0:T(8,128)} %bitcast.16, f32[8,4,128,128]{3,2,1,0:T(8,128)} %bitcast.15), custom_call_target="tpu_custom_call" | custom-call | tf_op jit(solution)/shard_map/collect/pallas_call | solution.py:431
  181.5 4.5 %join.1 = f32[512,1024]{1,0:T(8,128)} custom-call(f32[4,8,128,128]{3,2,1,0:T(8,128)} %get-tuple-element.19.b_ref, f32[8,4,128,128]{3,2,1,0:T(8,128)} %get-tuple-element.20.a_ref), custom_call_target="tpu_custom_call" | custom-call | tf_op jit(solution)/shard_map/join/pallas_call | solution.py:441
  (1 shorter events, 0.0 us)
Async XLA Ops:
  130.1 1.4 copy-start
  131.5 1.3 copy-start.1

commit v2 on v1

v2 whole, which is shorter than its diff:
```python
import functools

import jax
import jax.numpy as jnp
from jax import lax
from jax.experimental import pallas as pl
from jax.experimental.pallas import tpu as pltpu
from jax.sharding import PartitionSpec as P

MESH = pl.DeviceIdType.MESH
ANY = pl.BlockSpec(memory_space=pl.ANY)


def place():
    return lax.axis_index("row"), lax.axis_index("col"), lax.axis_index("layer")


def plane_peer(sizes, row, col, offset):
    rows, cols, _ = sizes
    down, right = offset // cols, offset % cols
    to = (lax.rem(row + down, rows), lax.rem(col + right, cols))
    source = lax.rem(row + rows - down, rows) * cols + lax.rem(col + cols - right, cols)
    return to, source


def greet(sizes):
    rows, cols, layers = sizes
    row, col, layer = place()
    barrier = pltpu.get_barrier_semaphore()
    for k in range(1, layers):
        to = (row, col, lax.rem(layer + k, layers))
        pl.semaphore_signal(barrier, inc=1, device_id=to, device_id_type=MESH)
    for offset in range(1, rows * cols):
        to, _ = plane_peer(sizes, row, col, offset)
        pl.semaphore_signal(barrier, inc=1, device_id=(*to, layer), device_id_type=MESH)
    pl.semaphore_wait(barrier, layers - 1 + rows * cols - 1)


def remote(src, dst, send_sem, recv_sem, to):
    return pltpu.make_async_remote_copy(
        src_ref=src,
        dst_ref=dst,
        send_sem=send_sem,
        recv_sem=recv_sem,
        device_id=to,
        device_id_type=MESH,
    )


def exchange(sizes, by_layer, by_plane, to_layer, to_plane, sems):
    rows, cols, layers = sizes
    row, col, layer = place()
    layer_send, layer_recv, plane_send, plane_recv = sems
    over_layer, over_plane = [], []
    for k in range(1, layers):
        other = lax.rem(layer + k, layers)
        over_layer.append(
            remote(
                by_layer.at[other],
                to_layer.at[layer],
                layer_send.at[k],
                layer_recv.at[k],
                (row, col, other),
            )
        )
    me = row * cols + col
    for offset in range(1, rows * cols):
        to, _ = plane_peer(sizes, row, col, offset)
        over_plane.append(
            remote(
                by_plane.at[to[0] * cols + to[1]],
                to_plane.at[me],
                plane_send.at[offset],
                plane_recv.at[offset],
                (*to, layer),
            )
        )
    return over_layer, over_plane


def halves(values):
    high = values.astype(jnp.bfloat16)
    low = (values - high.astype(jnp.float32)).astype(jnp.bfloat16)
    return high, low


def prepare(z_ref, x_ref, y_ref, block):
    alpha_rows = x_ref.shape[1]
    for ref, low_row in ((x_ref, 0), (z_ref, alpha_rows)):
        per = ref.shape[2] // block
        count = ref.shape[1]
        for j in range(y_ref.shape[0]):
            part = ref[j // per, :, (j % per) * block : (j % per + 1) * block]
            high, low = halves(part)
            y_ref[j, low_row : low_row + count, :block] = high
            y_ref[j, low_row : low_row + count, block:] = low


def multiply(piece, all_ref, names_ref, keep_ref, y_ref, sums_ref):
    _, share, block, _ = all_ref.shape
    group = 8 if share % 8 == 0 else 1

    def body(at, carry):
        results = []
        for i in range(group):
            n = at * group + i
            high, low = halves(all_ref[piece, n])
            weights = jnp.concatenate(
                [jnp.concatenate([high, high], axis=1), jnp.concatenate([low, low], axis=1)], axis=0
            )
            picked = y_ref[names_ref[piece, lax.div(n, 128), lax.rem(n, 128)]]
            both = lax.dot_general(
                picked, weights, (((1,), (1,)), ((), ())), preferred_element_type=jnp.float32
            )
            results.append(both[:, :block] + both[:, block:])
        running = sums_ref[at * group]
        for i in range(group):
            n = at * group + i
            running = results[i] + keep_ref[piece * share + n] * running
            sums_ref[n + 1] = running
        return carry

    lax.fori_loop(0, share // group, body, 0)


def gather(piece, last_ref, found_ref, sums_ref, a_ref, b_ref):
    alpha_rows = a_ref.shape[2]
    per_a, per_b = a_ref.shape[1], b_ref.shape[1]
    blocks = a_ref.shape[0] * per_a

    def body(i, carry):
        part = found_ref[piece * blocks + i] * sums_ref[last_ref[piece * blocks + i]]
        a_ref[lax.div(i, per_a), lax.rem(i, per_a)] += part[:alpha_rows]
        b_ref[lax.div(i, per_b), lax.rem(i, per_b)] += part[alpha_rows:]
        return carry

    lax.fori_loop(0, blocks, body, 0)


def sigma_kernel(
    sizes,
    c_ref,
    t_ref,
    h_ref,
    k_ref,
    keep_ref,
    last_ref,
    found_ref,
    beta_ref,
    alpha_ref,
    cols_ref,
    z_ref,
    x_ref,
    all_ref,
    y_ref,
    sums_ref,
    b_ref,
    a_ref,
    names_ref,
    own_sem,
    back_layer_send,
    back_layer_recv,
    back_plane_send,
    back_plane_recv,
    layer_send,
    layer_recv,
    plane_send,
    plane_recv,
    cols_send,
    cols_recv,
    rise_send,
    fall_send,
    relay_recv,
    chip_send,
    chip_recv,
    pair_send,
    pair_recv,
):
    rows, cols, layers = sizes
    row, col, layer = place()
    me = row * cols + col
    step = 2 if cols % 2 == 0 else 1
    offsets = [d * cols + e for d in range(rows) for e in range(0, cols, step)]
    share, block, _ = h_ref.shape
    size = share // (rows * cols)
    half = size // 2
    square = rows == 2 and cols == 4 and half > 0

    def piece_at(piece, source):
        return all_ref.at[piece, pl.ds(pl.multiple_of(source * size, size), size)]

    greet(sizes)

    def relay(piece, up):
        mine = h_ref.at[pl.ds(pl.multiple_of(me * size, size), size)]
        src = mine if piece is None else piece_at(piece, me)
        piece = layer if piece is None else piece
        sem = rise_send if up else fall_send
        to = (row, col, layer + 1 if up else layer - 1)
        return remote(src, piece_at(piece, me), sem.at[piece], relay_recv.at[piece], to)

    def to_chip(piece, at):
        to, _ = plane_peer(sizes, row, col, offsets[at])
        return remote(
            piece_at(piece, me),
            piece_at(piece, me),
            chip_send.at[piece, at],
            chip_recv.at[piece, at],
            (*to, layer),
        )

    def to_corner(piece, part):
        _, source = plane_peer(sizes, row, col, offsets[1 + part])
        to, _ = plane_peer(sizes, row, col, offsets[2 - part])
        first = pl.multiple_of(source * size + part * half, half)
        part_ref = all_ref.at[piece, pl.ds(first, half)]
        at = 0 if part == 0 else 3
        sems = chip_send.at[piece, at], chip_recv.at[piece, at]
        return remote(part_ref, part_ref, *sems, (*to, layer))

    def to_pair(piece, at):
        _, source = plane_peer(sizes, row, col, offsets[at])
        twin = (row, col + 1 - 2 * lax.rem(col, 2), layer)
        return remote(
            piece_at(piece, source),
            piece_at(piece, source),
            pair_send.at[piece, at],
            pair_recv.at[piece, at],
            twin,
        )

    chips = [1, 2] if square else list(range(1, len(offsets)))

    def each_piece(k, act):
        @pl.when(layer >= k)
        def below():
            act(layer - k, True)

        @pl.when(layer + k < layers)
        def above():
            act(layer + k, False)

    can_rise, can_fall = layer + 1 < layers, layer > 0

    @pl.when(can_rise)
    def rise():
        relay(None, True).start()

    @pl.when(can_fall)
    def fall():
        relay(None, False).start()

    over_layer, over_plane = exchange(
        sizes, c_ref, t_ref, z_ref, x_ref, (layer_send, layer_recv, plane_send, plane_recv)
    )
    names = []
    for k in range(1, layers):
        to = (row, col, lax.rem(layer + k, layers))
        names.append(remote(k_ref, cols_ref.at[layer], cols_send.at[k], cols_recv.at[k], to))
    own = [
        pltpu.make_async_copy(c_ref.at[layer], z_ref.at[layer], own_sem.at[0]),
        pltpu.make_async_copy(t_ref.at[me], x_ref.at[me], own_sem.at[1]),
        pltpu.make_async_copy(k_ref, cols_ref.at[layer], own_sem.at[2]),
        pltpu.make_async_copy(h_ref, all_ref.at[layer], own_sem.at[3]),
    ]
    for copy in names + over_plane + own:
        copy.start()

    def arrive(piece, upward):
        relay(piece, upward).wait_recv()

        @pl.when(can_rise if upward else can_fall)
        def onward():
            relay(piece, upward).start()

        for at in chips:
            to_chip(piece, at).start()
        if step == 2:
            to_pair(piece, 0).start()

    def pass_on(piece, upward):
        for at in chips:
            to_chip(piece, at).wait_recv()
            if square:
                to_corner(piece, at - 1).start()
            if step == 2:
                to_pair(piece, at).start()

    def pass_corner(piece, upward):
        if square:
            to_corner(piece, 0).wait_recv()
            to_corner(piece, 1).wait_recv()
            to_pair(piece, 3).start()

    early = min(2, layers - 1)
    for k in range(1, layers):
        each_piece(k, arrive)
        if k == early:
            for copy in over_layer:
                copy.start()
        if k > 1 and k < layers - 1:
            each_piece(k - 1, pass_on)
    if layers > 2:
        each_piece(layers - 2, pass_on)
    for k in range(1, layers - 2):
        each_piece(k, pass_corner)
    if layers > 1:
        each_piece(layers - 1, pass_on)
    if layers > 2:
        each_piece(layers - 2, pass_corner)

    for copy in names + over_plane + own[:3]:
        copy.wait()
    to_scalars = pltpu.make_async_copy(cols_ref, names_ref, own_sem.at[4])
    to_scalars.start()
    for copy in over_layer:
        copy.wait()
    prepare(z_ref, x_ref, y_ref, block)
    a_ref[...] = jnp.zeros_like(a_ref)
    b_ref[...] = jnp.zeros_like(b_ref)
    sums_ref[0] = jnp.zeros_like(sums_ref[0])
    to_scalars.wait()
    own[3].wait()

    sign = 1 - 2 * lax.div(2 * layer, layers)

    def treat(t, carry):
        piece = lax.rem(layer + layers + t * sign, layers)

        if step == 2:

            @pl.when(t > 0)
            def complete():
                for at in range(len(offsets)):
                    to_pair(piece, at).wait_recv()

        multiply(piece, all_ref, names_ref, keep_ref, y_ref, sums_ref)
        gather(piece, last_ref, found_ref, sums_ref, a_ref, b_ref)

        @pl.when(t == 0)
        def corners():
            if layers > 1:
                each_piece(layers - 1, pass_corner)

        return carry

    lax.fori_loop(0, layers, treat, 0)

    sems = (back_layer_send, back_layer_recv, back_plane_send, back_plane_recv)
    back_layer, back_plane = exchange(sizes, b_ref, a_ref, beta_ref, alpha_ref, sems)
    keep = [
        pltpu.make_async_copy(b_ref.at[layer], beta_ref.at[layer], own_sem.at[5]),
        pltpu.make_async_copy(a_ref.at[me], alpha_ref.at[me], own_sem.at[6]),
    ]
    for copy in back_layer + back_plane + keep:
        copy.start()

    def finish(piece, upward):
        @pl.when(can_rise if upward else can_fall)
        def sent():
            relay(piece, upward).wait_send()

        for at in chips:
            to_chip(piece, at).wait_send()
        if square:
            to_corner(piece, 0).wait_send()
            to_corner(piece, 1).wait_send()
        if step == 2:
            for at in range(len(offsets)):
                to_pair(piece, at).wait_send()

    for k in range(1, layers):
        each_piece(k, finish)

    @pl.when(can_rise)
    def risen():
        relay(None, True).wait_send()

    @pl.when(can_fall)
    def fallen():
        relay(None, False).wait_send()

    for copy in back_layer + back_plane + keep:
        copy.wait()


def join_kernel(b_ref, a_ref, out_ref):
    block = b_ref.shape[-1]
    for p in range(b_ref.shape[1]):
        out_ref[:, p * block : (p + 1) * block] = b_ref[0, p] + a_ref[p, 0].T


def local(sizes, coeffs, hblocks, hcount, hcols):
    rows, cols, layers = sizes
    group = rows * cols
    row_count, col_count = coeffs.shape
    share, block, _ = hblocks.shape
    stored = share * layers
    blocks = row_count * group // block
    alpha_rows, beta_rows = col_count // group, row_count // layers
    per_layer, per_plane = blocks // layers, blocks // group
    beta_back = (layers, per_layer, beta_rows, block)
    alpha_back = (group, per_plane, alpha_rows, block)
    f32 = jnp.float32
    dma = pltpu.SemaphoreType.DMA

    row_end = jnp.cumsum(hcount)
    index = jnp.arange(stored, dtype=jnp.int32)
    owners = jnp.sum((row_end[None, :] <= index[:, None]).astype(jnp.int32), axis=1)
    keep = jnp.concatenate([jnp.zeros((1,), bool), owners[1:] == owners[:-1]])
    keep = (keep & (index % share != 0)).astype(f32)
    base = jnp.arange(layers, dtype=jnp.int32)[:, None] * share
    ends = jnp.minimum(row_end[None, :], base + share) - base
    starts = jnp.maximum((row_end - hcount)[None, :], base) - base
    found = (ends > starts).astype(f32).reshape(-1)
    last = jnp.clip(ends, 1, share).reshape(-1)

    padded = -(-share // 1024) * 1024
    names = jnp.pad(hcols, (0, padded - share)).reshape(-1, 128)
    flipped = coeffs.T.reshape(group, alpha_rows, row_count)
    chips = group // 2 if cols % 2 == 0 else group
    smem = pl.BlockSpec(memory_space=pltpu.SMEM)
    beta, alpha, _ = pl.pallas_call(
        functools.partial(sigma_kernel, sizes),
        out_shape=(
            jax.ShapeDtypeStruct(beta_back, f32),
            jax.ShapeDtypeStruct(alpha_back, f32),
            jax.ShapeDtypeStruct((layers, *names.shape), jnp.int32),
        ),
        in_specs=[ANY] * 4 + [smem] * 3,
        out_specs=(ANY,) * 3,
        scratch_shapes=[
            pltpu.VMEM((layers, beta_rows, col_count), f32),
            pltpu.VMEM((group, alpha_rows, row_count), f32),
            pltpu.VMEM((layers, share, block, block), f32),
            pltpu.VMEM((blocks, alpha_rows + beta_rows, 2 * block), jnp.bfloat16),
            pltpu.VMEM((share + 1, alpha_rows + beta_rows, block), f32),
            pltpu.VMEM(beta_back, f32),
            pltpu.VMEM(alpha_back, f32),
            pltpu.SMEM((layers, *names.shape), jnp.int32),
            dma((7,)),
        ]
        + ([dma((layers,))] * 2 + [dma((group,))] * 2) * 2
        + [dma((layers,))] * 5
        + [dma((layers, chips))] * 4,
        compiler_params=pltpu.CompilerParams(
            collective_id=0, has_side_effects=True, vmem_limit_bytes=56 * 2**20
        ),
        name="sigma",
    )(
        coeffs.reshape(layers, beta_rows, col_count),
        flipped,
        hblocks,
        names,
        keep,
        last,
        found,
    )
    if alpha_rows == block and beta_rows == block:
        return pl.pallas_call(
            join_kernel,
            out_shape=jax.ShapeDtypeStruct((row_count, col_count), f32),
            grid=(layers,),
            in_specs=[
                pl.BlockSpec((1, per_layer, block, block), lambda i: (i, 0, 0, 0)),
                pl.BlockSpec((group, 1, block, block), lambda i: (0, i, 0, 0)),
            ],
            out_specs=pl.BlockSpec((block, col_count), lambda i: (i, 0)),
            name="join",
        )(beta, alpha)
    beta = beta.transpose(0, 2, 1, 3).reshape(row_count, col_count)
    alpha = alpha.transpose(1, 3, 0, 2).reshape(row_count, col_count)
    return beta + alpha


def solution(mesh):
    sizes = tuple(mesh.shape[name] for name in ("row", "col", "layer"))
    in_specs = (P(("row", "col"), "layer"), P("layer", None, None), P(), P("layer"))
    out_specs = P(("row", "col"), "layer")
    return jax.shard_map(
        functools.partial(local, sizes),
        mesh=mesh,
        in_specs=in_specs,
        out_specs=out_specs,
        check_vma=False,
    )
```

time: 187 us -> 158 us (0.84)
  Pallas kernels: 177 us -> 150 us
  local copies, waits for them, and re-layouts: 8.34 us -> 5.19 us
  other arithmetic: 0.26 us -> 2.77 us
    pallas_call x3 -> x1, Pallas kernels: 173 us -> 145 us  [local(): pl.pallas_call(functools.partial(sigma_kernel, sizes), out_shape=(jax.Sha...]
    unnamed x5 -> x0, local copies, waits for them, and re-layouts: 3.39 us -> none
where the time goes in v2:
time: 158 us
  Pallas kernels  150 us (95%)
  local copies, waits for them, and re-layouts  5.19 us (3%)
  other arithmetic  2.77 us (2%)
    pallas_call x1, Pallas kernels, local(): pl.pallas_call(functools.partial(sigma_kernel, sizes), out_shape=(jax.Sha...  145 us
    pallas_call x1, Pallas kernels, local(): pl.pallas_call(join_kernel, out_shape=jax.ShapeDtypeStruct((row_count, co...  4.48 us

profile of v2, /device:TPU:26, one launch (start us, length us, event | category | flops | bytes accessed | tf_op | source)
XLA Modules:
  0.0 157.6 jit_solution(10213836973414256175)
XLA Ops:
  0.0 0.1 sub.30
  0.1 0.1 sub.31
  0.2 1.2 pad_bitcast_fusion.k_ref
  1.4 0.7 copy.10
  2.2 0.1 reduce-window.8
  2.2 0.1 reduce
  2.3 0.7 sub.33
  3.0 0.1 convert_reduce_fusion
  3.1 0.1 slice_compare_fusion
  3.2 0.7 fusion.keep_ref
  3.8 0.1 broadcast_minimum_fusion
  3.9 0.1 min.29
  4.0 0.5 broadcast_clamp_fusion.last_ref
  4.5 0.1 max.22
  4.6 0.5 compare_convert_fusion.found_ref
  5.1 2.9 %copy.9 = f32[1024,512]{1,0:T(8,128)} copy(f32[1024,512]{0,1:T(8,128)} %bitcast.6) | data formatting | bytes 4194304 | tf_op jit(solution)/shard_map/transpose | solution.py:420
  8.0 145.2 %sigma.1 = (f32[4,8,128,128]{3,2,1,0:T(8,128)}, f32[8,4,128,128]{3,2,1,0:T(8,128)}, s32[4,8,128]{2,1,0:T(8,128)}) custom-call(f32[4,128,1024]{2,1,0:T(8,128)} %bitcast.7, f32[8,128,512]{2,1,0:T(8,128)} %bitcast.8, f32[64,128,128]{2,1,0:T(8,128)} %h_ref.1, s32[8,128]{1,0:T(8,128)} %pad_bitcast_fusion.k_ref, f32[256]{0:T(256)} %fusion.keep_ref, ...), custom_call_target="tpu_custom_call" | custom-call | tf_op jit(solution)/shard_map/sigma/pallas_call | solution.py:423
  153.2 4.5 %join.1 = f32[512,1024]{1,0:T(8,128)} custom-call(f32[4,8,128,128]{3,2,1,0:T(8,128)} %get-tuple-element.7.b_ref, f32[8,4,128,128]{3,2,1,0:T(8,128)} %get-tuple-element.8.a_ref), custom_call_target="tpu_custom_call" | custom-call | tf_op jit(solution)/shard_map/join/pallas_call | solution.py:460
  (3 shorter events, 0.0 us)

commit v3 on v2

--- a/solution.py
+++ b/solution.py
@@ -56,7 +56,7 @@
         other = lax.rem(layer + k, layers)
         over_layer.append(
             remote(
-                by_layer.at[other],
+                by_layer(other),
                 to_layer.at[layer],
                 layer_send.at[k],
                 layer_recv.at[k],
@@ -68,7 +68,7 @@
         to, _ = plane_peer(sizes, row, col, offset)
         over_plane.append(
             remote(
-                by_plane.at[to[0] * cols + to[1]],
+                by_plane(to[0] * cols + to[1]),
                 to_plane.at[me],
                 plane_send.at[offset],
                 plane_recv.at[offset],
@@ -84,19 +84,47 @@
     return high, low
 
 
-def prepare(z_ref, x_ref, y_ref, block):
-    alpha_rows = x_ref.shape[1]
-    for ref, low_row in ((x_ref, 0), (z_ref, alpha_rows)):
-        per = ref.shape[2] // block
-        count = ref.shape[1]
-        for j in range(y_ref.shape[0]):
-            part = ref[j // per, :, (j % per) * block : (j % per + 1) * block]
-            high, low = halves(part)
-            y_ref[j, low_row : low_row + count, :block] = high
-            y_ref[j, low_row : low_row + count, block:] = low
-
-
-def multiply(piece, all_ref, names_ref, keep_ref, y_ref, sums_ref):
+def turn(held_ref, turned_ref):
+    layers, width, block = turned_ref.shape
+    for i in range(layers):
+        for j in range(width // block):
+            part = held_ref[i * block : (i + 1) * block, j * block : (j + 1) * block]
+            turned_ref[i, j * block : (j + 1) * block, :] = part.T
+
+
+def mark(count_ref, keep_ref, share):
+    blocks = count_ref.shape[0]
+
+    def body(n, carry):
+        row, end = carry
+        opens = n == end
+        row = jnp.minimum(jnp.where(opens, row + 1, row), blocks - 1)
+        end = jnp.where(opens, end + count_ref[row], end)
+        keep_ref[n] = jnp.where(opens | (lax.rem(n, share) == 0), 0.0, 1.0)
+        return row, end
+
+    lax.fori_loop(0, keep_ref.shape[0], body, (jnp.int32(0), count_ref[0]))
+
+
+def prepare(wide, ref, y_ref, block, beta):
+    blocks = y_ref.shape[0]
+    if wide:
+        per = ref.shape[1] // block
+        side = slice(block, 2 * block) if beta else slice(0, block)
+        for j in range(blocks):
+            high, low = halves(ref[j // per, (j % per) * block : (j % per + 1) * block, :])
+            y_ref[j, :block, side] = high
+            y_ref[j, block:, side] = low
+        return
+    per, count = ref.shape[2] // block, ref.shape[1]
+    first = y_ref.shape[1] - count if beta else 0
+    for j in range(blocks):
+        high, low = halves(ref[j // per, :, (j % per) * block : (j % per + 1) * block])
+        y_ref[j, first : first + count, :block] = high
+        y_ref[j, first : first + count, block:] = low
+
+
+def multiply(wide, piece, all_ref, names_ref, keep_ref, y_ref, sums_ref):
     _, share, block, _ = all_ref.shape
     group = 8 if share % 8 == 0 else 1
 
@@ -105,14 +133,18 @@
         for i in range(group):
             n = at * group + i
             high, low = halves(all_ref[piece, n])
-            weights = jnp.concatenate(
+            four = jnp.concatenate(
                 [jnp.concatenate([high, high], axis=1), jnp.concatenate([low, low], axis=1)], axis=0
             )
-            picked = y_ref[names_ref[piece, lax.div(n, 128), lax.rem(n, 128)]]
-            both = lax.dot_general(
-                picked, weights, (((1,), (1,)), ((), ())), preferred_element_type=jnp.float32
-            )
-            results.append(both[:, :block] + both[:, block:])
+            picked = y_ref[names_ref[piece, 0, n]]
+            if wide:
+                both = jnp.dot(four, picked, preferred_element_type=jnp.float32)
+                results.append(both[:block] + both[block:])
+            else:
+                both = lax.dot_general(
+                    picked, four, (((1,), (1,)), ((), ())), preferred_element_type=jnp.float32
+                )
+                results.append(both[:, :block] + both[:, block:])
         running = sums_ref[at * group]
         for i in range(group):
             n = at * group + i
@@ -123,29 +155,33 @@
     lax.fori_loop(0, share // group, body, 0)
 
 
-def gather(piece, last_ref, found_ref, sums_ref, a_ref, b_ref):
-    alpha_rows = a_ref.shape[2]
+def gather(wide, piece, share, count_ref, sums_ref, a_ref, b_ref):
+    alpha_rows, block = a_ref.shape[2:]
     per_a, per_b = a_ref.shape[1], b_ref.shape[1]
-    blocks = a_ref.shape[0] * per_a
-
-    def body(i, carry):
-        part = found_ref[piece * blocks + i] * sums_ref[last_ref[piece * blocks + i]]
-        a_ref[lax.div(i, per_a), lax.rem(i, per_a)] += part[:alpha_rows]
-        b_ref[lax.div(i, per_b), lax.rem(i, per_b)] += part[alpha_rows:]
-        return carry
-
-    lax.fori_loop(0, blocks, body, 0)
+    base = piece * share
+
+    def body(i, start):
+        end = start + count_ref[i]
+        low, high = jnp.maximum(start, base), jnp.minimum(end, base + share)
+        found = jnp.where(high > low, 1.0, 0.0)
+        part = found * sums_ref[jnp.clip(high - base, 1, share)]
+        for_a = part[:, :block] if wide else part[:alpha_rows]
+        for_b = part[:, block:] if wide else part[alpha_rows:]
+        a_ref[lax.div(i, per_a), lax.rem(i, per_a)] += for_a
+        b_ref[lax.div(i, per_b), lax.rem(i, per_b)] += for_b
+        return end
+
+    lax.fori_loop(0, count_ref.shape[0], body, jnp.int32(0))
 
 
 def sigma_kernel(
     sizes,
+    wide,
     c_ref,
     t_ref,
     h_ref,
     k_ref,
-    keep_ref,
-    last_ref,
-    found_ref,
+    count_ref,
     beta_ref,
     alpha_ref,
     cols_ref,
@@ -157,6 +193,9 @@
     b_ref,
     a_ref,
     names_ref,
+    keep_ref,
+    held_ref,
+    turned_ref,
     own_sem,
     back_layer_send,
     back_layer_recv,
@@ -186,6 +225,14 @@
     half = size // 2
     square = rows == 2 and cols == 4 and half > 0
 
+    def for_layer(i):
+        return turned_ref.at[i] if wide else c_ref.at[i]
+
+    def for_plane(i):
+        if wide:
+            return t_ref.at[:, pl.ds(pl.multiple_of(i * block, block), block)]
+        return t_ref.at[i]
+
     def piece_at(piece, source):
         return all_ref.at[piece, pl.ds(pl.multiple_of(source * size, size), size)]
 
@@ -251,20 +298,28 @@
         relay(None, False).start()
 
     over_layer, over_plane = exchange(
-        sizes, c_ref, t_ref, z_ref, x_ref, (layer_send, layer_recv, plane_send, plane_recv)
+        sizes, for_layer, for_plane, z_ref, x_ref, (layer_send, layer_recv, plane_send, plane_recv)
     )
     names = []
     for k in range(1, layers):
         to = (row, col, lax.rem(layer + k, layers))
         names.append(remote(k_ref, cols_ref.at[layer], cols_send.at[k], cols_recv.at[k], to))
     own = [
-        pltpu.make_async_copy(c_ref.at[layer], z_ref.at[layer], own_sem.at[0]),
-        pltpu.make_async_copy(t_ref.at[me], x_ref.at[me], own_sem.at[1]),
+        pltpu.make_async_copy(for_layer(layer), z_ref.at[layer], own_sem.at[0]),
+        pltpu.make_async_copy(for_plane(me), x_ref.at[me], own_sem.at[1]),
         pltpu.make_async_copy(k_ref, cols_ref.at[layer], own_sem.at[2]),
         pltpu.make_async_copy(h_ref, all_ref.at[layer], own_sem.at[3]),
     ]
-    for copy in names + over_plane + own:
+    if wide:
+        held = pltpu.make_async_copy(c_ref, held_ref, own_sem.at[7])
+        held.start()
+    for copy in names + over_plane + own[1:]:
         copy.start()
+    if wide:
+        held.wait()
+        turn(held_ref, turned_ref)
+    own[0].start()
+    mark(count_ref, keep_ref, share)
 
     def arrive(piece, upward):
         relay(piece, upward).wait_recv()
@@ -311,14 +366,15 @@
 
     for copy in names + over_plane + own[:3]:
         copy.wait()
+    prepare(wide, x_ref, y_ref, block, False)
+    a_ref[...] = jnp.zeros_like(a_ref)
+    b_ref[...] = jnp.zeros_like(b_ref)
+    sums_ref[0] = jnp.zeros_like(sums_ref[0])
     to_scalars = pltpu.make_async_copy(cols_ref, names_ref, own_sem.at[4])
     to_scalars.start()
     for copy in over_layer:
         copy.wait()
-    prepare(z_ref, x_ref, y_ref, block)
-    a_ref[...] = jnp.zeros_like(a_ref)
-    b_ref[...] = jnp.zeros_like(b_ref)
-    sums_ref[0] = jnp.zeros_like(sums_ref[0])
+    prepare(wide, z_ref, y_ref, block, True)
     to_scalars.wait()
     own[3].wait()
 
@@ -334,8 +390,8 @@
                 for at in range(len(offsets)):
                     to_pair(piece, at).wait_recv()
 
-        multiply(piece, all_ref, names_ref, keep_ref, y_ref, sums_ref)
-        gather(piece, last_ref, found_ref, sums_ref, a_ref, b_ref)
+        multiply(wide, piece, all_ref, names_ref, keep_ref, y_ref, sums_ref)
+        gather(wide, piece, share, count_ref, sums_ref, a_ref, b_ref)
 
         @pl.when(t == 0)
         def corners():
@@ -347,7 +403,9 @@
     lax.fori_loop(0, layers, treat, 0)
 
     sems = (back_layer_send, back_layer_recv, back_plane_send, back_plane_recv)
-    back_layer, back_plane = exchange(sizes, b_ref, a_ref, beta_ref, alpha_ref, sems)
+    back_layer, back_plane = exchange(
+        sizes, lambda i: b_ref.at[i], lambda i: a_ref.at[i], beta_ref, alpha_ref, sems
+    )
     keep = [
         pltpu.make_async_copy(b_ref.at[layer], beta_ref.at[layer], own_sem.at[5]),
         pltpu.make_async_copy(a_ref.at[me], alpha_ref.at[me], own_sem.at[6]),
@@ -387,7 +445,7 @@
 def join_kernel(b_ref, a_ref, out_ref):
     block = b_ref.shape[-1]
     for p in range(b_ref.shape[1]):
-        out_ref[:, p * block : (p + 1) * block] = b_ref[0, p] + a_ref[p, 0].T
+        out_ref[:, p * block : (p + 1) * block] = b_ref[0, p].T + a_ref[p, 0]
 
 
 def local(sizes, coeffs, hblocks, hcount, hcols):
@@ -404,41 +462,44 @@
     f32 = jnp.float32
     dma = pltpu.SemaphoreType.DMA
 
-    row_end = jnp.cumsum(hcount)
-    index = jnp.arange(stored, dtype=jnp.int32)
-    owners = jnp.sum((row_end[None, :] <= index[:, None]).astype(jnp.int32), axis=1)
-    keep = jnp.concatenate([jnp.zeros((1,), bool), owners[1:] == owners[:-1]])
-    keep = (keep & (index % share != 0)).astype(f32)
-    base = jnp.arange(layers, dtype=jnp.int32)[:, None] * share
-    ends = jnp.minimum(row_end[None, :], base + share) - base
-    starts = jnp.maximum((row_end - hcount)[None, :], base) - base
-    found = (ends > starts).astype(f32).reshape(-1)
-    last = jnp.clip(ends, 1, share).reshape(-1)
-
-    padded = -(-share // 1024) * 1024
-    names = jnp.pad(hcols, (0, padded - share)).reshape(-1, 128)
-    flipped = coeffs.T.reshape(group, alpha_rows, row_count)
+    wide = alpha_rows == block and beta_rows == block
+    names = hcols.reshape(1, share)
+    if wide:
+        for_layer, for_plane = coeffs, coeffs
+        z_shape, x_shape = (layers, col_count, block), (group, row_count, block)
+        y_shape, sum_shape = (blocks, 2 * block, 2 * block), (share + 1, block, 2 * block)
+        held, turned = coeffs.shape, z_shape
+    else:
+        for_layer = coeffs.reshape(layers, beta_rows, col_count)
+        for_plane = coeffs.T.reshape(group, alpha_rows, row_count)
+        z_shape, x_shape = for_layer.shape, for_plane.shape
+        both = alpha_rows + beta_rows
+        y_shape, sum_shape = (blocks, both, 2 * block), (share + 1, both, block)
+        held = turned = (8, 128)
     chips = group // 2 if cols % 2 == 0 else group
     smem = pl.BlockSpec(memory_space=pltpu.SMEM)
     beta, alpha, _ = pl.pallas_call(
-        functools.partial(sigma_kernel, sizes),
+        functools.partial(sigma_kernel, sizes, wide),
         out_shape=(
             jax.ShapeDtypeStruct(beta_back, f32),
             jax.ShapeDtypeStruct(alpha_back, f32),
             jax.ShapeDtypeStruct((layers, *names.shape), jnp.int32),
         ),
-        in_specs=[ANY] * 4 + [smem] * 3,
+        in_specs=[ANY] * 4 + [smem],
         out_specs=(ANY,) * 3,
         scratch_shapes=[
-            pltpu.VMEM((layers, beta_rows, col_count), f32),
-            pltpu.VMEM((group, alpha_rows, row_count), f32),
+            pltpu.VMEM(z_shape, f32),
+            pltpu.VMEM(x_shape, f32),
             pltpu.VMEM((layers, share, block, block), f32),
-            pltpu.VMEM((blocks, alpha_rows + beta_rows, 2 * block), jnp.bfloat16),
-            pltpu.VMEM((share + 1, alpha_rows + beta_rows, block), f32),
+            pltpu.VMEM(y_shape, jnp.bfloat16),
+            pltpu.VMEM(sum_shape, f32),
             pltpu.VMEM(beta_back, f32),
             pltpu.VMEM(alpha_back, f32),
             pltpu.SMEM((layers, *names.shape), jnp.int32),
-            dma((7,)),
+            pltpu.SMEM((stored,), f32),
+            pltpu.VMEM(held, f32),
+            pltpu.VMEM(turned, f32),
+            dma((8,)),
         ]
         + ([dma((layers,))] * 2 + [dma((group,))] * 2) * 2
         + [dma((layers,))] * 5
@@ -448,15 +509,13 @@
         ),
         name="sigma",
     )(
-        coeffs.reshape(layers, beta_rows, col_count),
-        flipped,
+        for_layer,
+        for_plane,
         hblocks,
         names,
-        keep,
-        last,
-        found,
+        hcount,
     )
-    if alpha_rows == block and beta_rows == block:
+    if wide:
         return pl.pallas_call(
             join_kernel,
             out_shape=jax.ShapeDtypeStruct((row_count, col_count), f32),

time: 158 us -> 149 us (0.943)
  local copies, waits for them, and re-layouts: 5.19 us -> 0 us
  other arithmetic: 2.77 us -> 0 us
    transpose x1 -> x0, local copies, waits for them, and re-layouts: 2.88 us -> none  [local(): flipped = coeffs.T.reshape(group, alpha_rows, row_count)]
where the time goes in v3:
time: 149 us
  Pallas kernels  149 us (100%)
    pallas_call x1, Pallas kernels, local(): pl.pallas_call(functools.partial(sigma_kernel, sizes, wide), out_shape=(j...  145 us
    pallas_call x1, Pallas kernels, local(): pl.pallas_call(join_kernel, out_shape=jax.ShapeDtypeStruct((row_count, co...  4.48 us

profile of v3, /device:TPU:26, one launch (start us, length us, event | category | flops | bytes accessed | tf_op | source)
XLA Modules:
  0.0 149.1 jit_solution(5615323108829633214)
XLA Ops:
  0.0 144.6 %sigma.1 = (f32[4,8,128,128]{3,2,1,0:T(8,128)}, f32[8,4,128,128]{3,2,1,0:T(8,128)}, s32[4,1,64]{2,1,0:T(1,128)}) custom-call(f32[512,1024]{1,0:T(8,128)} %t_ref.1, f32[512,1024]{1,0:T(8,128)} %t_ref.1, f32[64,128,128]{2,1,0:T(8,128)} %h_ref.1, s32[1,64]{1,0:T(1,128)} %bitcast.1, s32[32]{0:T(128)} %count_ref.1), custom_call_target="tpu_custom_call" | custom-call | tf_op jit(solution)/shard_map/sigma/pallas_call | solution.py:481
  144.6 4.5 %join.1 = f32[512,1024]{1,0:T(8,128)} custom-call(f32[4,8,128,128]{3,2,1,0:T(8,128)} %get-tuple-element.7.b_ref, f32[8,4,128,128]{3,2,1,0:T(8,128)} %get-tuple-element.8.a_ref), custom_call_target="tpu_custom_call" | custom-call | tf_op jit(solution)/shard_map/join/pallas_call | solution.py:519

commit v4 on v3

--- a/solution.py
+++ b/solution.py
@@ -106,22 +106,21 @@
     lax.fori_loop(0, keep_ref.shape[0], body, (jnp.int32(0), count_ref[0]))
 
 
-def prepare(wide, ref, y_ref, block, beta):
-    blocks = y_ref.shape[0]
+def prepare(wide, ref, i, y_ref, block, beta):
     if wide:
         per = ref.shape[1] // block
         side = slice(block, 2 * block) if beta else slice(0, block)
-        for j in range(blocks):
-            high, low = halves(ref[j // per, (j % per) * block : (j % per + 1) * block, :])
-            y_ref[j, :block, side] = high
-            y_ref[j, block:, side] = low
+        for j in range(per):
+            high, low = halves(ref[i, j * block : (j + 1) * block, :])
+            y_ref[i * per + j, :block, side] = high
+            y_ref[i * per + j, block:, side] = low
         return
     per, count = ref.shape[2] // block, ref.shape[1]
     first = y_ref.shape[1] - count if beta else 0
-    for j in range(blocks):
-        high, low = halves(ref[j // per, :, (j % per) * block : (j % per + 1) * block])
-        y_ref[j, first : first + count, :block] = high
-        y_ref[j, first : first + count, block:] = low
+    for j in range(per):
+        high, low = halves(ref[i, :, j * block : (j + 1) * block])
+        y_ref[i * per + j, first : first + count, :block] = high
+        y_ref[i * per + j, first : first + count, block:] = low
 
 
 def multiply(wide, piece, all_ref, names_ref, keep_ref, y_ref, sums_ref):
@@ -129,7 +128,7 @@
     group = 8 if share % 8 == 0 else 1
 
     def body(at, carry):
-        results = []
+        running = sums_ref[at * group]
         for i in range(group):
             n = at * group + i
             high, low = halves(all_ref[piece, n])
@@ -139,16 +138,13 @@
             picked = y_ref[names_ref[piece, 0, n]]
             if wide:
                 both = jnp.dot(four, picked, preferred_element_type=jnp.float32)
-                results.append(both[:block] + both[block:])
+                result = both[:block] + both[block:]
             else:
                 both = lax.dot_general(
                     picked, four, (((1,), (1,)), ((), ())), preferred_element_type=jnp.float32
                 )
-                results.append(both[:, :block] + both[:, block:])
-        running = sums_ref[at * group]
-        for i in range(group):
-            n = at * group + i
-            running = results[i] + keep_ref[piece * share + n] * running
+                result = both[:, :block] + both[:, block:]
+            running = result + keep_ref[piece * share + n] * running
             sums_ref[n + 1] = running
         return carry
 
@@ -214,6 +210,7 @@
     chip_recv,
     pair_send,
     pair_recv,
+    out_ref=None,
 ):
     rows, cols, layers = sizes
     row, col, layer = place()
@@ -366,15 +363,17 @@
 
     for copy in names + over_plane + own[:3]:
         copy.wait()
-    prepare(wide, x_ref, y_ref, block, False)
+    for i in range(rows * cols):
+        prepare(wide, x_ref, i, y_ref, block, False)
+    prepare(wide, z_ref, layer, y_ref, block, True)
     a_ref[...] = jnp.zeros_like(a_ref)
     b_ref[...] = jnp.zeros_like(b_ref)
     sums_ref[0] = jnp.zeros_like(sums_ref[0])
     to_scalars = pltpu.make_async_copy(cols_ref, names_ref, own_sem.at[4])
     to_scalars.start()
-    for copy in over_layer:
+    for k, copy in enumerate(over_layer, 1):
         copy.wait()
-    prepare(wide, z_ref, y_ref, block, True)
+        prepare(wide, z_ref, lax.rem(layer + layers - k, layers), y_ref, block, True)
     to_scalars.wait()
     own[3].wait()
 
@@ -438,14 +437,24 @@
     def fallen():
         relay(None, False).wait_send()
 
-    for copy in back_layer + back_plane + keep:
+    for copy in back_plane + keep:
         copy.wait()
 
-
-def join_kernel(b_ref, a_ref, out_ref):
-    block = b_ref.shape[-1]
-    for p in range(b_ref.shape[1]):
-        out_ref[:, p * block : (p + 1) * block] = b_ref[0, p].T + a_ref[p, 0]
+    def join(i):
+        for p in range(rows * cols):
+            at = pl.ds(pl.multiple_of(i * block, block), block)
+            out_ref[at, p * block : (p + 1) * block] = beta_ref[i, p].T + alpha_ref[p, i]
+
+    if wide:
+        join(layer)
+    for k, copy in enumerate(back_layer, 1):
+        copy.wait()
+        if wide:
+            join(lax.rem(layer + layers - k, layers))
+
+
+def wide_kernel(sizes, c, t, h, k, count, out_ref, columns, beta, alpha, *scratch):
+    sigma_kernel(sizes, True, c, t, h, k, count, beta, alpha, columns, *scratch, out_ref=out_ref)
 
 
 def local(sizes, coeffs, hblocks, hcount, hcols):
@@ -478,16 +487,28 @@
         held = turned = (8, 128)
     chips = group // 2 if cols % 2 == 0 else group
     smem = pl.BlockSpec(memory_space=pltpu.SMEM)
-    beta, alpha, _ = pl.pallas_call(
-        functools.partial(sigma_kernel, sizes, wide),
-        out_shape=(
+    gathered = jax.ShapeDtypeStruct((layers, *names.shape), jnp.int32)
+    if wide:
+        kernel = functools.partial(wide_kernel, sizes)
+        out_shape = (jax.ShapeDtypeStruct((row_count, col_count), f32), gathered)
+        out_specs = (pl.BlockSpec(memory_space=pltpu.VMEM), ANY)
+        landing = [pltpu.VMEM(beta_back, f32), pltpu.VMEM(alpha_back, f32)]
+    else:
+        kernel = functools.partial(sigma_kernel, sizes, False)
+        out_shape = (
             jax.ShapeDtypeStruct(beta_back, f32),
             jax.ShapeDtypeStruct(alpha_back, f32),
-            jax.ShapeDtypeStruct((layers, *names.shape), jnp.int32),
-        ),
+            gathered,
+        )
+        out_specs = (ANY,) * 3
+        landing = []
+    results = pl.pallas_call(
+        kernel,
+        out_shape=out_shape,
         in_specs=[ANY] * 4 + [smem],
-        out_specs=(ANY,) * 3,
-        scratch_shapes=[
+        out_specs=out_specs,
+        scratch_shapes=landing
+        + [
             pltpu.VMEM(z_shape, f32),
             pltpu.VMEM(x_shape, f32),
             pltpu.VMEM((layers, share, block, block), f32),
@@ -516,17 +537,8 @@
         hcount,
     )
     if wide:
-        return pl.pallas_call(
-            join_kernel,
-            out_shape=jax.ShapeDtypeStruct((row_count, col_count), f32),
-            grid=(layers,),
-            in_specs=[
-                pl.BlockSpec((1, per_layer, block, block), lambda i: (i, 0, 0, 0)),
-                pl.BlockSpec((group, 1, block, block), lambda i: (0, i, 0, 0)),
-            ],
-            out_specs=pl.BlockSpec((block, col_count), lambda i: (i, 0)),
-            name="join",
-        )(beta, alpha)
+        return results[0]
+    beta, alpha, _ = results
     beta = beta.transpose(0, 2, 1, 3).reshape(row_count, col_count)
     alpha = alpha.transpose(1, 3, 0, 2).reshape(row_count, col_count)
     return beta + alpha

time: 149 us -> 150 us (level)
  local copies, waits for them, and re-layouts: 0 us -> 3.16 us
  Pallas kernels: 149 us -> 146 us
    unnamed x0 -> x1, local copies, waits for them, and re-layouts: none -> 3.16 us
    pallas_call x2 -> x1, Pallas kernels: 149 us -> 146 us  [local(): pl.pallas_call(kernel, out_shape=out_shape, in_specs=[ANY] * 4 + [smem],...]
where the time goes in v4:
time: 150 us; the launch traced here: 149 us
  Pallas kernels  146 us (97%)
  local copies, waits for them, and re-layouts  3.16 us (2%)
    pallas_call x1, Pallas kernels, local(): pl.pallas_call(kernel, out_shape=out_shape, in_specs=[ANY] * 4 + [smem],...  146 us
    unnamed x1, local copies, waits for them, and re-layouts  3.16 us

profile of v4, /device:TPU:26, one launch (start us, length us, event | category | flops | bytes accessed | tf_op | source)
XLA Modules:
  0.0 149.4 jit_solution(1312722741360880721)
XLA Ops:
  0.0 146.2 %sigma.1 = (f32[512,1024]{1,0:T(8,128)}, s32[4,1,64]{2,1,0:T(1,128)}) custom-call(f32[512,1024]{1,0:T(8,128)} %t.1, f32[512,1024]{1,0:T(8,128)} %t.1, f32[64,128,128]{2,1,0:T(8,128)} %h.1, s32[1,64]{1,0:T(1,128)} %bitcast.1, s32[32]{0:T(128)} %count.1), custom_call_target="tpu_custom_call" | custom-call | tf_op jit(solution)/shard_map/sigma/pallas_call | solution.py:505
  146.2 3.2 %copy.6 = f32[512,1024]{1,0:T(8,128)} copy(f32[512,1024]{1,0:T(8,128)} %get-tuple-element.6) | data formatting | bytes 4194304

commit v5 on v4

--- a/solution.py
+++ b/solution.py
@@ -190,7 +190,6 @@
     a_ref,
     names_ref,
     keep_ref,
-    held_ref,
     turned_ref,
     own_sem,
     back_layer_send,
@@ -212,6 +211,7 @@
     pair_recv,
     out_ref=None,
 ):
+    held_ref = out_ref
     rows, cols, layers = sizes
     row, col, layer = place()
     me = row * cols + col
@@ -344,14 +344,20 @@
             to_corner(piece, 1).wait_recv()
             to_pair(piece, 3).start()
 
+    def start_layer(inner):
+        for k, copy in enumerate(over_layer, 1):
+            other = lax.rem(layer + k, layers)
+            outer = (other == 0) | (other == layers - 1)
+            pl.when(jnp.logical_not(outer) if inner else outer)(copy.start)
+
     early = min(2, layers - 1)
     for k in range(1, layers):
         each_piece(k, arrive)
         if k == early:
-            for copy in over_layer:
-                copy.start()
+            start_layer(True)
         if k > 1 and k < layers - 1:
             each_piece(k - 1, pass_on)
+    start_layer(False)
     if layers > 2:
         each_piece(layers - 2, pass_on)
     for k in range(1, layers - 2):
@@ -477,14 +483,14 @@
         for_layer, for_plane = coeffs, coeffs
         z_shape, x_shape = (layers, col_count, block), (group, row_count, block)
         y_shape, sum_shape = (blocks, 2 * block, 2 * block), (share + 1, block, 2 * block)
-        held, turned = coeffs.shape, z_shape
+        turned = z_shape
     else:
         for_layer = coeffs.reshape(layers, beta_rows, col_count)
         for_plane = coeffs.T.reshape(group, alpha_rows, row_count)
         z_shape, x_shape = for_layer.shape, for_plane.shape
         both = alpha_rows + beta_rows
         y_shape, sum_shape = (blocks, both, 2 * block), (share + 1, both, block)
-        held = turned = (8, 128)
+        turned = (8, 128)
     chips = group // 2 if cols % 2 == 0 else group
     smem = pl.BlockSpec(memory_space=pltpu.SMEM)
     gathered = jax.ShapeDtypeStruct((layers, *names.shape), jnp.int32)
@@ -518,7 +524,6 @@
             pltpu.VMEM(alpha_back, f32),
             pltpu.SMEM((layers, *names.shape), jnp.int32),
             pltpu.SMEM((stored,), f32),
-            pltpu.VMEM(held, f32),
             pltpu.VMEM(turned, f32),
             dma((8,)),
         ]
@@ -526,7 +531,7 @@
         + [dma((layers,))] * 5
         + [dma((layers, chips))] * 4,
         compiler_params=pltpu.CompilerParams(
-            collective_id=0, has_side_effects=True, vmem_limit_bytes=56 * 2**20
+            collective_id=0, has_side_effects=True, vmem_limit_bytes=48 * 2**20
         ),
         name="sigma",
     )(

time: 150 us -> 154 us (1.027)
  Pallas kernels: 146 us -> 148 us
    pallas_call x1, Pallas kernels: 146 us -> 148 us  [local(): pl.pallas_call(kernel, out_shape=out_shape, in_specs=[ANY] * 4 + [smem],...]
    unnamed x1 -> x7, local copies, waits for them, and re-layouts: 3.16 us -> 4.22 us
where the time goes in v5:
time: 154 us; the launch traced here: 152 us
  Pallas kernels  148 us (96%)
  local copies, waits for them, and re-layouts  4.22 us (3%)
    pallas_call x1, Pallas kernels, local(): pl.pallas_call(kernel, out_shape=out_shape, in_specs=[ANY] * 4 + [smem],...  148 us
    unnamed x7, local copies, waits for them, and re-layouts  4.22 us

profile of v5, /device:TPU:26, one launch (start us, length us, event | category | flops | bytes accessed | tf_op | source)
XLA Modules:
  0.0 152.3 jit_solution(10598004450997073025)
XLA Ops:
  0.0 0.0 copy-start
  0.0 1.6 %copy-done = f32[512,1024]{1,0:T(8,128)S(1)} copy-done((f32[512,1024]{1,0:T(8,128)S(1)}, f32[512,1024]{1,0:T(8,128)}, u32[]{:S(2)}) %copy-start) | copy-done | bytes 2097176
  1.6 0.0 copy-start.1
  1.6 0.7 copy-done.1
  2.2 0.0 copy-start.2
  2.2 0.7 copy-done.2
  2.9 148.1 %sigma.1 = (f32[512,1024]{1,0:T(8,128)S(1)}, s32[4,1,64]{2,1,0:T(1,128)}) custom-call(f32[512,1024]{1,0:T(8,128)S(1)} %copy-done, f32[512,1024]{1,0:T(8,128)S(1)} %copy-done, f32[64,128,128]{2,1,0:T(8,128)} %h.1, s32[1,64]{1,0:T(1,128)S(1)} %bitcast.1, s32[32]{0:T(128)S(1)} %copy-done.2), custom_call_target="tpu_custom_call" | custom-call | tf_op jit(solution)/shard_map/sigma/pallas_call | solution.py:511
  151.0 1.3 copy.6
Async XLA Ops:
  0.0 1.6 %copy-start = (f32[512,1024]{1,0:T(8,128)S(1)}, f32[512,1024]{1,0:T(8,128)}, u32[]{:S(2)}) copy-start(f32[512,1024]{1,0:T(8,128)} %t.1) | copy-start | bytes 6291460
  1.6 0.7 copy-start.1
  2.2 0.7 copy-start.2

commit v6 on v4

--- a/solution.py
+++ b/solution.py
@@ -123,19 +123,24 @@
         y_ref[i * per + j, first : first + count, block:] = low
 
 
-def multiply(wide, piece, all_ref, names_ref, keep_ref, y_ref, sums_ref):
+def lanes_of(side, block):
+    return {"alpha": slice(0, block), "beta": slice(block, 2 * block), "both": slice(None)}[side]
+
+
+def multiply(wide, side, piece, all_ref, names_ref, keep_ref, y_ref, sums_ref):
     _, share, block, _ = all_ref.shape
     group = 8 if share % 8 == 0 else 1
+    lanes = lanes_of(side, block)
 
     def body(at, carry):
-        running = sums_ref[at * group]
+        running = sums_ref[at * group, :, lanes]
         for i in range(group):
             n = at * group + i
             high, low = halves(all_ref[piece, n])
             four = jnp.concatenate(
                 [jnp.concatenate([high, high], axis=1), jnp.concatenate([low, low], axis=1)], axis=0
             )
-            picked = y_ref[names_ref[piece, 0, n]]
+            picked = y_ref[names_ref[piece, 0, n], :, lanes]
             if wide:
                 both = jnp.dot(four, picked, preferred_element_type=jnp.float32)
                 result = both[:block] + both[block:]
@@ -145,13 +150,13 @@
                 )
                 result = both[:, :block] + both[:, block:]
             running = result + keep_ref[piece * share + n] * running
-            sums_ref[n + 1] = running
+            sums_ref[n + 1, :, lanes] = running
         return carry
 
     lax.fori_loop(0, share // group, body, 0)
 
 
-def gather(wide, piece, share, count_ref, sums_ref, a_ref, b_ref):
+def gather(wide, side, piece, share, count_ref, sums_ref, a_ref, b_ref):
     alpha_rows, block = a_ref.shape[2:]
     per_a, per_b = a_ref.shape[1], b_ref.shape[1]
     base = piece * share
@@ -160,11 +165,17 @@
         end = start + count_ref[i]
         low, high = jnp.maximum(start, base), jnp.minimum(end, base + share)
         found = jnp.where(high > low, 1.0, 0.0)
-        part = found * sums_ref[jnp.clip(high - base, 1, share)]
-        for_a = part[:, :block] if wide else part[:alpha_rows]
-        for_b = part[:, block:] if wide else part[alpha_rows:]
-        a_ref[lax.div(i, per_a), lax.rem(i, per_a)] += for_a
-        b_ref[lax.div(i, per_b), lax.rem(i, per_b)] += for_b
+        part = found * sums_ref[jnp.clip(high - base, 1, share), :, lanes_of(side, block)]
+        if side != "both":
+            for_a = for_b = part
+        elif wide:
+            for_a, for_b = part[:, :block], part[:, block:]
+        else:
+            for_a, for_b = part[:alpha_rows], part[alpha_rows:]
+        if side != "beta":
+            a_ref[lax.div(i, per_a), lax.rem(i, per_a)] += for_a
+        if side != "alpha":
+            b_ref[lax.div(i, per_b), lax.rem(i, per_b)] += for_b
         return end
 
     lax.fori_loop(0, count_ref.shape[0], body, jnp.int32(0))
@@ -344,7 +355,7 @@
             to_corner(piece, 1).wait_recv()
             to_pair(piece, 3).start()
 
-    early = min(2, layers - 1)
+    early = 1
     for k in range(1, layers):
         each_piece(k, arrive)
         if k == early:
@@ -371,35 +382,43 @@
     sums_ref[0] = jnp.zeros_like(sums_ref[0])
     to_scalars = pltpu.make_async_copy(cols_ref, names_ref, own_sem.at[4])
     to_scalars.start()
+    to_scalars.wait()
+    own[3].wait()
+    sign = 1 - 2 * lax.div(2 * layer, layers)
+
+    def piece_of(t):
+        return lax.rem(layer + layers + t * sign, layers)
+
+    def complete(t):
+        if step == 2:
+            for at in range(len(offsets)):
+                to_pair(piece_of(t), at).wait_recv()
+
+    def work(t, side):
+        piece = piece_of(t)
+        multiply(wide, side, piece, all_ref, names_ref, keep_ref, y_ref, sums_ref)
+        gather(wide, side, piece, share, count_ref, sums_ref, a_ref, b_ref)
+
+    ahead = 2 if wide and layers > 2 else 0
+    for t in range(ahead):
+        if t > 0:
+            complete(t)
+        work(t, "alpha")
     for k, copy in enumerate(over_layer, 1):
         copy.wait()
         prepare(wide, z_ref, lax.rem(layer + layers - k, layers), y_ref, block, True)
-    to_scalars.wait()
-    own[3].wait()
-
-    sign = 1 - 2 * lax.div(2 * layer, layers)
+    work(0, "beta" if ahead > 0 else "both")
+    if layers > 1:
+        each_piece(layers - 1, pass_corner)
+    if ahead > 1:
+        work(1, "beta")
 
     def treat(t, carry):
-        piece = lax.rem(layer + layers + t * sign, layers)
-
-        if step == 2:
-
-            @pl.when(t > 0)
-            def complete():
-                for at in range(len(offsets)):
-                    to_pair(piece, at).wait_recv()
-
-        multiply(wide, piece, all_ref, names_ref, keep_ref, y_ref, sums_ref)
-        gather(wide, piece, share, count_ref, sums_ref, a_ref, b_ref)
-
-        @pl.when(t == 0)
-        def corners():
-            if layers > 1:
-                each_piece(layers - 1, pass_corner)
-
+        complete(t)
+        work(t, "both")
         return carry
 
-    lax.fori_loop(0, layers, treat, 0)
+    lax.fori_loop(max(1, ahead), layers, treat, 0)
 
     sems = (back_layer_send, back_layer_recv, back_plane_send, back_plane_recv)
     back_layer, back_plane = exchange(

time: 150 us -> 162 us (1.080)
  Pallas kernels: 146 us -> 158 us
    pallas_call x1, Pallas kernels: 146 us -> 158 us  [local(): pl.pallas_call(kernel, out_shape=out_shape, in_specs=[ANY] * 4 + [smem],...]
where the time goes in v6:
time: 162 us; the launch traced here: 161 us
  Pallas kernels  158 us (98%)
  local copies, waits for them, and re-layouts  3.16 us (2%)
    pallas_call x1, Pallas kernels, local(): pl.pallas_call(kernel, out_shape=out_shape, in_specs=[ANY] * 4 + [smem],...  158 us

profile of v6, /device:TPU:26, one launch (start us, length us, event | category | flops | bytes accessed | tf_op | source)
XLA Modules:
  0.0 160.9 jit_solution(2246789709729879767)
XLA Ops:
  0.0 157.7 %sigma.1 = (f32[512,1024]{1,0:T(8,128)}, s32[4,1,64]{2,1,0:T(1,128)}) custom-call(f32[512,1024]{1,0:T(8,128)} %t.1, f32[512,1024]{1,0:T(8,128)} %t.1, f32[64,128,128]{2,1,0:T(8,128)} %h.1, s32[1,64]{1,0:T(1,128)} %bitcast.1, s32[32]{0:T(128)} %count.1), custom_call_target="tpu_custom_call" | custom-call | tf_op jit(solution)/shard_map/sigma/pallas_call | solution.py:524
  157.7 3.2 %copy.6 = f32[512,1024]{1,0:T(8,128)} copy(f32[512,1024]{1,0:T(8,128)} %get-tuple-element.6) | data formatting | bytes 4194304

commit v7 on v6

--- a/solution.py
+++ b/solution.py
@@ -355,7 +355,7 @@
             to_corner(piece, 1).wait_recv()
             to_pair(piece, 3).start()
 
-    early = 1
+    early = min(2, layers - 1)
     for k in range(1, layers):
         each_piece(k, arrive)
         if k == early:
@@ -399,7 +399,7 @@
         multiply(wide, side, piece, all_ref, names_ref, keep_ref, y_ref, sums_ref)
         gather(wide, side, piece, share, count_ref, sums_ref, a_ref, b_ref)
 
-    ahead = 2 if wide and layers > 2 else 0
+    ahead = 1 if wide else 0
     for t in range(ahead):
         if t > 0:
             complete(t)

time: 162 us -> 153 us (0.944)
  Pallas kernels: 158 us -> 150 us
    pallas_call x1, Pallas kernels: 158 us -> 150 us  [local(): pl.pallas_call(kernel, out_shape=out_shape, in_specs=[ANY] * 4 + [smem],...]
where the time goes in v7:
time: 153 us
  Pallas kernels  150 us (98%)
  local copies, waits for them, and re-layouts  3.16 us (2%)
    pallas_call x1, Pallas kernels, local(): pl.pallas_call(kernel, out_shape=out_shape, in_specs=[ANY] * 4 + [smem],...  150 us
    unnamed x1, local copies, waits for them, and re-layouts  3.16 us

profile of v7, /device:TPU:26, one launch (start us, length us, event | category | flops | bytes accessed | tf_op | source)
XLA Modules:
  0.0 153.1 jit_solution(10601422965573497823)
XLA Ops:
  0.0 149.9 %sigma.1 = (f32[512,1024]{1,0:T(8,128)}, s32[4,1,64]{2,1,0:T(1,128)}) custom-call(f32[512,1024]{1,0:T(8,128)} %t.1, f32[512,1024]{1,0:T(8,128)} %t.1, f32[64,128,128]{2,1,0:T(8,128)} %h.1, s32[1,64]{1,0:T(1,128)} %bitcast.1, s32[32]{0:T(128)} %count.1), custom_call_target="tpu_custom_call" | custom-call | tf_op jit(solution)/shard_map/sigma/pallas_call | solution.py:524
  149.9 3.2 %copy.6 = f32[512,1024]{1,0:T(8,128)} copy(f32[512,1024]{1,0:T(8,128)} %get-tuple-element.6) | data formatting | bytes 4194304
